TPU v7x, 32 devices: a whole 2x2x4 slice. The times are simulated.
32 devices in a mesh: rows: 8 (over z, x), modes: 4 (over y, core).
Axes of the slice: x: 2, y: 2, z: 4, core: 2. Of those that a mesh axis runs over, the one named last changes fastest.
Arguments:
- snapshots: bfloat16 [1024, 5, 6144], P(None, None, 'rows')
- eigvec: bfloat16 [1024, 256], P('rows', 'modes'), may hold values from -0.1875 to 0.1875
- eigval: float32 [256], replicated, may hold values from 30720 to 245760
- jac_self: bfloat16 [5, 5, 6144], P(None, None, 'rows'), may hold values from -0.5 to 1.5
- jac_off: bfloat16 [6, 5, 5, 6144], P(None, None, None, 'rows'), may hold values from -1 to 1
- neighbor: int32 [6, 6144], P(None, 'rows'), may hold values from 0 to 1279
- send_list: int32 [2, 2048], P(None, 'rows'), may hold values from 0 to 767
- send_count: int32 [2, 8], P(None, 'rows'), may hold values from 1 to 256
- owned_cells: int32 [8], P('rows'), may hold values from 1 to 768, 4608 in all
Outputs:
- test_basis: bfloat16 [256, 5, 6144], P('modes', None, 'rows')
- reduced: float32 [256, 256], P('rows', 'modes')
Inputs may be any that keep to these rules, and one draw needn't show every extreme that they name: neighbor[b, c] indexes the extended slots of the cell's own partition: its 768 own slots, then 256 lower ghost slots, then 256 upper ghost slots. `send_list`: entries of partition p's lists are local slots of partition p.
All inputs are finite; a program needn't handle non-finite values. No bound on the sum of `owned_cells` on one device may be relied on, other than what follows from the above.
Results may differ from a plain program's by a relative error of at most 0.0049.
Values may be sent and summed in bfloat16 or wider, within the bound.
A program may use at most 128 MiB of HBM per device.

v0:
```python
import jax
import jax.numpy as jnp
from jax import lax
from jax.sharding import PartitionSpec as P


def passed_along(value, axis, steps):
    count = lax.axis_size(axis)
    first, last = (max(0, -steps), min(count, count - steps))
    return lax.ppermute(value, axis, [(source, source + steps) for source in range(first, last)])


def neighbour_rows(piece, offset):
    return passed_along(piece, "rows", offset)


def shards(
    snapshots, eigvec, eigval, jac_self, jac_off, neighbor, send_list, send_count, owned_cells
):
    snap_count, var_count, cell_count = snapshots.shape
    panel_width = eigvec.shape[1]
    halo_slots = send_list.shape[1]
    snap_rows = snapshots.reshape(snap_count, var_count * cell_count)
    modes_sum = lax.dot_general(
        lax.all_gather(eigvec, "rows", axis=0, tiled=True),
        snap_rows,
        (((0,), (0,)), ((), ())),
        preferred_element_type=jnp.float32,
    )
    owned_mask = jnp.arange(cell_count, dtype=jnp.int32)[None, None, :] < owned_cells[0]
    modes = jnp.where(
        owned_mask,
        modes_sum.reshape(panel_width, var_count, cell_count),
        jnp.zeros((), jnp.float32),
    ).astype(jnp.bfloat16)
    picked = jnp.take(modes, send_list.reshape(-1), axis=2).reshape(
        panel_width, var_count, 2, halo_slots
    )
    live_slots = jnp.arange(halo_slots, dtype=jnp.int32)[None, :] < send_count
    picked = jnp.where(live_slots[None, None], picked, jnp.zeros((), jnp.bfloat16))
    from_below = neighbour_rows(picked[:, :, 1], 1)
    from_above = neighbour_rows(picked[:, :, 0], -1)
    extended = jnp.concatenate([modes, from_below, from_above], axis=2)
    own_term = jnp.einsum("vwc,mwc->mvc", jac_self, modes, preferred_element_type=jnp.float32)
    neighbours = jnp.take(extended, neighbor, axis=2)
    off_term = jnp.einsum("bvwc,mwbc->mvc", jac_off, neighbours, preferred_element_type=jnp.float32)
    test_local = jnp.where(owned_mask, own_term + off_term, jnp.zeros((), jnp.float32)).astype(
        jnp.bfloat16
    )
    products = lax.dot_general(
        snap_rows,
        test_local.reshape(panel_width, var_count * cell_count),
        (((1,), (1,)), ((), ())),
        preferred_element_type=jnp.float32,
    )
    shares = lax.psum_scatter(products, "rows", scatter_dimension=0, tiled=True)
    eigvec_rows = lax.all_gather(eigvec, "modes", axis=1, tiled=True)
    partial_sum = jnp.dot(
        eigvec_rows.astype(jnp.float32).T, shares, precision=lax.Precision.HIGHEST
    )
    reduced_part = lax.psum_scatter(partial_sum, "rows", scatter_dimension=0, tiled=True)
    rows_out = reduced_part.shape[0]
    scales = 1.0 / jnp.sqrt(eigval)
    row_scales = lax.dynamic_slice_in_dim(scales, lax.axis_index("rows") * rows_out, rows_out, 0)
    col_scales = lax.dynamic_slice_in_dim(
        scales, lax.axis_index("modes") * panel_width, panel_width, 0
    )
    reduced = reduced_part * row_scales[:, None] * col_scales[None, :]
    return (test_local, reduced)


def solution(mesh):
    in_specs = (
        P(None, None, "rows"),
        P("rows", "modes"),
        P(),
        P(None, None, "rows"),
        P(None, None, None, "rows"),
        P(None, "rows"),
        P(None, "rows"),
        P(None, "rows"),
        P("rows"),
    )
    out_specs = (P("modes", None, "rows"), P("rows", "modes"))
    return jax.shard_map(shards, mesh=mesh, in_specs=in_specs, out_specs=out_specs, check_vma=False)
```

profile of v0, /device:TPU:0, one launch (start us, length us, event | category | flops | bytes accessed | tf_op | source)
XLA Modules:
  0.0 272.5 jit_solution(6265888050190093898)
XLA Ops:
  7.9 10.7 %copy.30 = bf16[1024,5,768]{0,2,1:T(8,128)(2,1)} copy(bf16[1024,5,768]{2,0,1:T(8,128)(2,1)} %param.9) | data formatting | bytes 15728640 | tf_op args[0]
  18.6 27.9 %all_gather.6 = bf16[1024,64]{0,1:T(8,128)(2,1)S(1)} all-gather(bf16[128,64]{0,1:T(8,128)(2,1)S(1)} %copy-done.3), channel_id=1, replica_groups=mesh['rows'=8,'modes'=4] {'rows'}, dimensions={0}, use_global_device_ids=true | all-gather | bytes 147456 | tf_op jit(solution)/shard_map/all_gather | solution.py:25
  46.5 5.7 %fusion.8 = bf16[64,5,768]{2,0,1:T(8,128)(2,1)S(1)} fusion(bf16[1024,5,768]{0,2,1:T(8,128)(2,1)} %copy.30, pred[768]{0:T(1024)(128)(4,1)S(1)} %iota_compare_fusion, bf16[1024,64]{0,1:T(8,128)(2,1)S(1)} %all_gather.6), kind=kOutput, calls=%fused_computation.10 | convolution fusion | flops 503808000 | bytes 8487680 | tf_op jit(solution)/shard_map/dot_general | solution.py:24
  52.2 1.1 copy.31
  53.4 1.8 gather_fusion
  55.8 3.4 %collective-permute-start = (bf16[64,5,256]{2,0,1:T(8,128)(2,1)S(1)}, bf16[64,5,256]{2,0,1:T(8,128)(2,1)S(1)}, u32[]{:S(2)}, u32[]{:S(2)}) collective-permute-start(bf16[64,5,256]{2,0,1:T(8,128)(2,1)S(1)} %get-tuple-element.8), channel_id=1, source_target_pairs={{0,4},{4,8},{8,12},{12,16},{16,20},{20,24},{24,28},{1,5},{5,9},{9,... | collective-permute-start | bytes 491528 | tf_op jit(solution)/shard_map/ppermute | solution.py:10
  59.2 1.5 collective-permute-start.1
  60.8 6.7 %copy.39 = bf16[6,5,5,768]{0,1,2,3:T(8,128)(2,1)} copy(bf16[6,5,5,768]{3,0,2,1:T(8,128)(2,1)} %param.13) | data formatting | bytes 460800 | tf_op args[4]
  67.5 1.9 copy.32
  69.4 1.0 pad_maximum_fusion
  70.4 2.9 %copy.36 = bf16[64,5,1280]{0,1,2:T(8,128)(2,1)S(1)} copy(bf16[64,5,1280]{2,0,1:T(8,128)(2,1)S(1)} %pad_maximum_fusion) | data formatting | bytes 1638400 | tf_op jit(solution)/shard_map/concatenate | solution.py:43
  73.3 12.9 %gather_fusion.1 = bf16[4608,64,5]{1,2,0:T(8,128)(2,1)} fusion(bf16[64,5,1280]{0,1,2:T(8,128)(2,1)S(1)} %copy.36, s32[5120]{0:T(1024)S(1)} %pad_clamp_fusion), kind=kCustom, calls=%fused_computation.1 | custom fusion | bytes 5916672 | tf_op jit(solution)/shard_map/jit(_take)/gather | solution.py:45
  86.2 9.9 %copy.46 = bf16[6,768,64,5]{1,0,2,3:T(8,128)(2,1)} copy(bf16[6,768,64,5]{2,3,1,0:T(8,128)(2,1)} %bitcast.58) | data formatting | bytes 5898240 | tf_op jit(solution)/shard_map/jit(_take)/gather | solution.py:45
  96.1 4.5 %select_bitcast_fusion = bf16[64,5,6,768]{3,2,0,1:T(8,128)(2,1)} fusion(bf16[6,768,64,5]{1,0,2,3:T(8,128)(2,1)} %copy.46, pred[6,768]{1,0:T(8,128)(4,1)S(1)} %compare_and_fusion), kind=kLoop, calls=%fused_computation.4 | loop fusion | flops 1474560 | bytes 5902848 | tf_op jit(solution)/shard_map/jit(_take)/select_n | solution.py:45
  100.5 14.5 %copy.38 = bf16[64,5,6,768]{0,2,1,3:T(8,128)(2,1)} copy(bf16[64,5,6,768]{3,2,0,1:T(8,128)(2,1)} %select_bitcast_fusion) | data formatting | bytes 5898240 | tf_op jit(solution)/shard_map/jit(_take)/select_n | solution.py:45
  115.0 9.6 %fusion.12 = f32[768,64,5,1]{1,2,3,0:T(8,128)S(1)} fusion(bf16[64,5,6,768]{0,2,1,3:T(8,128)(2,1)} %copy.38, bf16[6,5,5,768]{0,1,2,3:T(8,128)(2,1)} %copy.39), kind=kOutput, calls=%fused_computation.28 | convolution fusion | flops 14745600 | bytes 4162560 | tf_op jit(solution)/shard_map/bvwc,mwbc->mvc/dot_general | solution.py:46
  124.7 5.0 %fusion.4 = bf16[64,5,768]{0,1,2:T(8,128)(2,1)} fusion(f32[768,64,5,1]{1,2,3,0:T(8,128)S(1)} %fusion.12, bf16[64,5,768]{0,1,2:T(8,128)(2,1)} %copy-done, bf16[5,5,768]{1,0,2:T(8,128)(2,1)} %copy.32, pred[768]{0:T(1024)(128)(4,1)S(1)} %iota_compare_fusion), kind=kOutput, calls=%fused_computation.8 | convolution fusion | flops 3194880 | bytes 2005248 | tf_op jit(solution)/shard_map/vwc,mwc->mvc/dot_general | solution.py:44
  129.7 1.8 copy.41
  131.5 6.6 %convolution_bitcast_fusion = f32[1024,64]{0,1:T(8,128)} fusion(bf16[64,5,768]{2,0,1:T(8,128)(2,1)S(1)} %copy.41, bf16[1024,5,768]{2,0,1:T(8,128)(2,1)} %param.9), kind=kOutput, calls=%fused_computation.11 | convolution fusion | flops 503316480 | bytes 8617984 | tf_op jit(solution)/shard_map/dot_general | solution.py:50
  138.2 5.2 %all_gather.7 = bf16[128,256]{0,1:T(8,128)(2,1)S(1)} all-gather(bf16[128,64]{0,1:T(8,128)(2,1)S(1)} %copy-done.3), channel_id=1, replica_groups=mesh['rows'=8,'modes'=4] {'modes'}, dimensions={1}, use_global_device_ids=true | all-gather | bytes 81920 | tf_op jit(solution)/shard_map/all_gather | solution.py:57
  143.4 57.5 %reduce-scatter.5.cloned.1.call-done = f32[128,64]{0,1:T(8,128)} async-done(((f32[1024,64]{0,1:T(8,128)}), f32[128,64]{0,1:T(8,128)}) %reduce-scatter.5.cloned.1.call-update) | async-done | bytes 32784 | tf_op jit(solution)/shard_map/reduce_scatter | solution.py:56
  200.9 1.0 convolution_bitcast_fusion.1
  202.8 61.3 %reduce-scatter.7.cloned.1.call-done = f32[32,64]{1,0:T(8,128)} async-done(((f32[256,64]{1,0:T(8,128)}), f32[32,64]{1,0:T(8,128)}) %reduce-scatter.7.cloned.1.call-update) | async-done | bytes 8208
  264.1 0.8 copy.48
  (40 shorter events, 2.5 us)
Async XLA Ops:
  7.2 193.7 %reduce-scatter.5.cloned.1.call-start = ((), (), s32[]{:S(2)}) async-start(), calls=%async_computation.2 | async-start | bytes 294912 | tf_op jit(solution)/shard_map/reduce_scatter | solution.py:56
  7.9 10.7 %copy-start.3 = (bf16[128,64]{0,1:T(8,128)(2,1)S(1)}, bf16[128,64]{0,1:T(8,128)(2,1)}, u32[]{:S(2)}) copy-start(bf16[128,64]{0,1:T(8,128)(2,1)} %param.10) | copy-start | bytes 49156
  46.5 6.9 %copy-start.5 = (s32[2,256]{1,0:T(2,128)S(1)}, s32[2,256]{1,0:T(2,128)}, u32[]{:S(2)}) copy-start(s32[2,256]{1,0:T(2,128)} %param.15) | copy-start | bytes 6148
  52.2 3.5 %copy-start.7 = (s32[2,1]{0,1:T(1,128)S(1)}, s32[2,1]{0,1:T(1,128)}, u32[]{:S(2)}) copy-start(s32[2,1]{0,1:T(1,128)} %param.16) | copy-start | bytes 28
  52.2 8.5 %copy-start.2 = (s32[6,768]{1,0:T(8,128)S(1)}, s32[6,768]{1,0:T(8,128)}, u32[]{:S(2)}) copy-start(s32[6,768]{1,0:T(8,128)} %param.14) | copy-start | bytes 55300
  53.3 14.2 %copy-start = (bf16[64,5,768]{0,1,2:T(8,128)(2,1)}, bf16[64,5,768]{0,1,2:T(8,128)(2,1)S(1)}, u32[]{:S(2)}) copy-start(bf16[64,5,768]{0,1,2:T(8,128)(2,1)S(1)} %copy.31) | copy-start | bytes 1474564
  55.8 13.6 %collective-permute-start = (bf16[64,5,256]{2,0,1:T(8,128)(2,1)S(1)}, bf16[64,5,256]{2,0,1:T(8,128)(2,1)S(1)}, u32[]{:S(2)}, u32[]{:S(2)}) collective-permute-start(bf16[64,5,256]{2,0,1:T(8,128)(2,1)S(1)} %get-tuple-element.8), channel_id=1, source_target_pairs={{0,4},{4,8},{8,12},{12,16},{16,20},{20,24},{24,28},{1,5},{5,9},{9,... | collective-permute-start | bytes 491528 | tf_op jit(solution)/shard_map/ppermute | solution.py:10
  59.2 10.2 %collective-permute-start.1 = (bf16[64,5,256]{2,0,1:T(8,128)(2,1)S(1)}, bf16[64,5,256]{2,0,1:T(8,128)(2,1)}, u32[]{:S(2)}, u32[]{:S(2)}) collective-permute-start(bf16[64,5,256]{2,0,1:T(8,128)(2,1)S(1)} %get-tuple-element.9), channel_id=1, source_target_pairs={{4,0},{8,4},{12,8},{16,12},{20,16},{24,20},{28,24},{5,1},{9,5},{13... | collective-permute-start | bytes 491528 | tf_op jit(solution)/shard_map/ppermute | solution.py:10
  60.8 6.7 %copy-start.4 = (bf16[5,5,768]{2,1,0:T(8,128)(2,1)S(1)}, bf16[5,5,768]{2,1,0:T(8,128)(2,1)}, u32[]{:S(2)}) copy-start(bf16[5,5,768]{2,1,0:T(8,128)(2,1)} %param.12) | copy-start | bytes 115204
  131.5 6.6 %copy-start.1 = (bf16[64,5,768]{2,0,1:T(8,128)(2,1)}, bf16[64,5,768]{2,0,1:T(8,128)(2,1)S(1)}, u32[]{:S(2)}) copy-start(bf16[64,5,768]{2,0,1:T(8,128)(2,1)S(1)} %copy.41) | copy-start | bytes 1474564
  131.5 71.2 %copy-start.6 = (f32[256]{0:T(256)S(1)}, f32[256]{0:T(256)}, u32[]{:S(2)}) copy-start(f32[256]{0:T(256)} %param.11) | copy-start | bytes 3076
  138.1 126.0 %reduce-scatter.7.cloned.1.call-start = ((), (), s32[]{:S(2)}) async-start(), calls=%async_computation.3 | async-start | bytes 147456
Sparse Core Ops, SparseCore 0:
  138.2 62.6 reduce-scatter.4
  204.2 59.8 reduce-scatter.6
where the time goes:
time: 274 us; the launch traced here: 273 us
  waiting for transfers between devices  119 us (43%)
  local copies, waits for them, and re-layouts  67.1 us (24%)
  blocking collectives  33.1 us (12%)
  matrix products  27.9 us (10%)
  between operations  14.9 us (5%)
  other arithmetic  5.69 us (2%)
  starting transfers between devices  4.97 us (2%)
    unnamed x3, waiting for transfers between devices  61.3 us
    reduce_scatter x1, waiting for transfers between devices, shards(): shares = lax.psum_scatter(products, 'rows', scatter_dimension=0, tiled=True)  57.5 us
    all_gather x1, blocking collectives, shards(): lax.all_gather(eigvec, 'rows', axis=0, tiled=True)  27.9 us
    unnamed x24, local copies, waits for them, and re-layouts  23.4 us
    gather x2, local copies, waits for them, and re-layouts, shards(): neighbours = jnp.take(extended, neighbor, axis=2)  22.8 us
    select_n x1, local copies, waits for them, and re-layouts, shards(): neighbours = jnp.take(extended, neighbor, axis=2)  14.5 us
    dot_general x1, matrix products, shards(): jnp.einsum('bvwc,mwbc->mvc', jac_off, neighbours, preferred_element_type=...  9.62 us
    dot_general x1, matrix products, shards(): lax.dot_general(snap_rows, test_local.reshape(panel_width, var_count * ce...  6.58 us
  transfers between devices with their start and end apart: 4, of which 2 were waited for; matrix products, arithmetic and copies ran while one was open for 3% of the time, Pallas kernels for 0%

commit v1 on v0

--- a/solution.py
+++ b/solution.py
@@ -2,6 +2,28 @@
 import jax.numpy as jnp
 from jax import lax
 from jax.sharding import PartitionSpec as P
+
+
+def laid_out(blocks, dim):
+    shape = list(blocks.shape[1:])
+    shape[dim] *= blocks.shape[0]
+    return jnp.moveaxis(blocks, 0, dim).reshape(shape)
+
+
+def collected_by_bits(value, axis):
+    peers = lax.axis_size(axis)
+    blocks = value[None]
+    for level in range(peers.bit_length() - 1):
+        apart = 1 << level
+        other = lax.ppermute(blocks, axis, [(i, i ^ apart) for i in range(peers)])
+        both = jnp.stack([blocks, other])
+        upper = lax.axis_index(axis) >> level & 1
+        blocks = jnp.where(upper == 0, both, both[::-1]).reshape(-1, *value.shape)
+    return blocks
+
+
+def gather_by_bits(x, axis, dim):
+    return laid_out(collected_by_bits(x, axis), dim)
 
 
 def passed_along(value, axis, steps):
@@ -22,7 +44,7 @@
     halo_slots = send_list.shape[1]
     snap_rows = snapshots.reshape(snap_count, var_count * cell_count)
     modes_sum = lax.dot_general(
-        lax.all_gather(eigvec, "rows", axis=0, tiled=True),
+        gather_by_bits(eigvec, "rows", 0),
         snap_rows,
         (((0,), (0,)), ((), ())),
         preferred_element_type=jnp.float32,

time: 274 us -> 260 us (0.949)
  blocking collectives: 33.1 us -> 5.25 us
  starting transfers between devices: 4.97 us -> 12.7 us
  waiting for transfers between devices: 119 us -> 122 us
    all_gather x1 -> x0, blocking collectives: 27.9 us -> none  [shards(): lax.all_gather(eigvec, 'rows', axis=0, tiled=True)]
    ppermute x0 -> x3, starting transfers between devices: none -> 7.55 us  [collected_by_bits(): other = lax.ppermute(blocks, axis, [(i, i ^ apart) for i in range(peers)])]
    ppermute x0 -> x3, waiting for transfers between devices: none -> 2.92 us  [collected_by_bits(): other = lax.ppermute(blocks, axis, [(i, i ^ apart) for i in range(peers)])]
    unnamed x24 -> x20, local copies, waits for them, and re-layouts: 23.4 us -> 24 us
  transfers between devices with their start and end apart: 4 -> 7, of which waited for: 2 -> 3; matrix products, arithmetic and copies ran while one was open for 3% -> 8% of each run, Pallas kernels for 0% -> 0%
where the time goes in v1:
time: 260 us; the launch traced here: 259 us
  waiting for transfers between devices  122 us (47%)
  local copies, waits for them, and re-layouts  67.9 us (26%)
  matrix products  27.9 us (11%)
  between operations  15 us (6%)
  starting transfers between devices  12.7 us (5%)
  other arithmetic  7.92 us (3%)
  blocking collectives  5.25 us (2%)
    unnamed x3, waiting for transfers between devices  61.3 us
    reduce_scatter x1, waiting for transfers between devices, shards(): shares = lax.psum_scatter(products, 'rows', scatter_dimension=0, tiled=True)  57.7 us
    unnamed x20, local copies, waits for them, and re-layouts  24 us
    gather x2, local copies, waits for them, and re-layouts, shards(): neighbours = jnp.take(extended, neighbor, axis=2)  22.8 us
    select_n x1, local copies, waits for them, and re-layouts, shards(): neighbours = jnp.take(extended, neighbor, axis=2)  14.5 us
    dot_general x1, matrix products, shards(): jnp.einsum('bvwc,mwbc->mvc', jac_off, neighbours, preferred_element_type=...  9.62 us
    ppermute x3, starting transfers between devices, collected_by_bits(): other = lax.ppermute(blocks, axis, [(i, i ^ apart) for i in range(peers)])  7.55 us
    dot_general x1, matrix products, shards(): lax.dot_general(snap_rows, test_local.reshape(panel_width, var_count * ce...  6.59 us
  transfers between devices with their start and end apart: 7, of which 3 were waited for; matrix products, arithmetic and copies ran while one was open for 8% of the time, Pallas kernels for 0%

profile of v1, /device:TPU:0, one launch (start us, length us, event | category | flops | bytes accessed | tf_op | source)
XLA Modules:
  0.0 258.6 jit_solution(13518248508554326904)
XLA Ops:
  7.2 3.0 %collective-permute-start = (bf16[1,128,64]{1,2,0:T(8,128)(2,1)}, bf16[1,128,64]{1,2,0:T(8,128)(2,1)S(1)}, u32[]{:S(2)}, u32[]{:S(2)}) collective-permute-start(bf16[1,128,64]{1,2,0:T(8,128)(2,1)} %bitcast.73), channel_id=1, source_target_pairs={{0,4},{4,0},{8,12},{12,8},{16,20},{20,16},{24,28},{28,24},{1,5},{5... | collective-permute-start | bytes 49160 | tf_op jit(solution)/shard_map/ppermute | solution.py:18
  13.2 1.9 collective-permute-start.1
  15.7 10.6 %copy.33 = bf16[1024,5,768]{0,2,1:T(8,128)(2,1)} copy(bf16[1024,5,768]{2,0,1:T(8,128)(2,1)} %param.9) | data formatting | bytes 15728640 | tf_op args[0]
  26.4 2.7 %collective-permute-start.2 = (bf16[4,128,64]{1,2,0:T(8,128)(2,1)S(1)}, bf16[4,128,64]{1,2,0:T(8,128)(2,1)S(1)}, u32[]{:S(2)}, u32[]{:S(2)}) collective-permute-start(bf16[4,128,64]{1,2,0:T(8,128)(2,1)S(1)} %bitcast.71), channel_id=1, source_target_pairs={{0,16},{4,20},{8,24},{12,28},{16,0},{20,4},{24,8},{28,12},{1,17},{... | collective-permute-start | bytes 196616 | tf_op jit(solution)/shard_map/ppermute | solution.py:18
  29.1 2.9 %collective-permute-done.2 = bf16[4,128,64]{1,2,0:T(8,128)(2,1)S(1)} collective-permute-done((bf16[4,128,64]{1,2,0:T(8,128)(2,1)S(1)}, bf16[4,128,64]{1,2,0:T(8,128)(2,1)S(1)}, u32[]{:S(2)}, u32[]{:S(2)}) %collective-permute-start.2) | collective-permute-done | bytes 65568 | tf_op jit(solution)/shard_map/ppermute | solution.py:18
  32.2 5.7 %fusion.8 = bf16[64,5,768]{2,0,1:T(8,128)(2,1)S(1)} fusion(bf16[1024,64,1]{0,1,2:T(8,128)(2,1)S(1)} %reshape.110, bf16[1024,5,768]{0,2,1:T(8,128)(2,1)} %copy.33, pred[768]{0:T(1024)(128)(4,1)S(1)} %iota_compare_fusion), kind=kOutput, calls=%fused_computation.10 | convolution fusion | flops 503808000 | bytes 8487680 | tf_op jit(solution)/shard_map/dot_general | solution.py:46
  37.9 1.1 copy.34
  39.1 1.8 gather_fusion
  41.4 3.6 %collective-permute-start.3 = (bf16[64,5,256]{2,0,1:T(8,128)(2,1)S(1)}, bf16[64,5,256]{2,0,1:T(8,128)(2,1)S(1)}, u32[]{:S(2)}, u32[]{:S(2)}) collective-permute-start(bf16[64,5,256]{2,0,1:T(8,128)(2,1)S(1)} %get-tuple-element.8), channel_id=1, source_target_pairs={{0,4},{4,8},{8,12},{12,16},{16,20},{20,24},{24,28},{1,5},{5,9},{9,... | collective-permute-start | bytes 491528 | tf_op jit(solution)/shard_map/ppermute | solution.py:32
  45.1 1.5 collective-permute-start.4
  46.6 6.7 %copy.42 = bf16[6,5,5,768]{0,1,2,3:T(8,128)(2,1)} copy(bf16[6,5,5,768]{3,0,2,1:T(8,128)(2,1)} %param.13) | data formatting | bytes 460800 | tf_op args[4]
  53.3 1.9 copy.35
  56.2 2.9 %copy.39 = bf16[64,5,1280]{0,1,2:T(8,128)(2,1)S(1)} copy(bf16[64,5,1280]{2,0,1:T(8,128)(2,1)S(1)} %pad_maximum_fusion) | data formatting | bytes 1638400 | tf_op jit(solution)/shard_map/concatenate | solution.py:65
  59.1 12.9 %gather_fusion.1 = bf16[4608,64,5]{1,2,0:T(8,128)(2,1)} fusion(bf16[64,5,1280]{0,1,2:T(8,128)(2,1)S(1)} %copy.39, s32[5120]{0:T(1024)S(1)} %pad_clamp_fusion), kind=kCustom, calls=%fused_computation.1 | custom fusion | bytes 5916672 | tf_op jit(solution)/shard_map/jit(_take)/gather | solution.py:67
  72.0 9.9 %copy.49 = bf16[6,768,64,5]{1,0,2,3:T(8,128)(2,1)} copy(bf16[6,768,64,5]{2,3,1,0:T(8,128)(2,1)} %bitcast.69) | data formatting | bytes 5898240 | tf_op jit(solution)/shard_map/jit(_take)/gather | solution.py:67
  81.9 4.5 %select_bitcast_fusion = bf16[64,5,6,768]{3,2,0,1:T(8,128)(2,1)} fusion(bf16[6,768,64,5]{1,0,2,3:T(8,128)(2,1)} %copy.49, pred[6,768]{1,0:T(8,128)(4,1)S(1)} %compare_and_fusion), kind=kLoop, calls=%fused_computation.4 | loop fusion | flops 1474560 | bytes 5902848 | tf_op jit(solution)/shard_map/jit(_take)/select_n | solution.py:67
  86.3 14.5 %copy.41 = bf16[64,5,6,768]{0,2,1,3:T(8,128)(2,1)} copy(bf16[64,5,6,768]{3,2,0,1:T(8,128)(2,1)} %select_bitcast_fusion) | data formatting | bytes 5898240 | tf_op jit(solution)/shard_map/jit(_take)/select_n | solution.py:67
  100.9 9.6 %fusion.13 = f32[768,64,5,1]{1,2,3,0:T(8,128)S(1)} fusion(bf16[64,5,6,768]{0,2,1,3:T(8,128)(2,1)} %copy.41, bf16[6,5,5,768]{0,1,2,3:T(8,128)(2,1)} %copy.42), kind=kOutput, calls=%fused_computation.35 | convolution fusion | flops 14745600 | bytes 4162560 | tf_op jit(solution)/shard_map/bvwc,mwbc->mvc/dot_general | solution.py:68
  110.5 5.0 %fusion.4 = bf16[64,5,768]{0,1,2:T(8,128)(2,1)} fusion(f32[768,64,5,1]{1,2,3,0:T(8,128)S(1)} %fusion.13, bf16[64,5,768]{0,1,2:T(8,128)(2,1)} %copy-done, bf16[5,5,768]{1,0,2:T(8,128)(2,1)} %copy.35, pred[768]{0:T(1024)(128)(4,1)S(1)} %iota_compare_fusion), kind=kOutput, calls=%fused_computation.8 | convolution fusion | flops 3194880 | bytes 2005248 | tf_op jit(solution)/shard_map/vwc,mwc->mvc/dot_general | solution.py:66
  115.5 1.8 copy.44
  117.4 6.6 %convolution_bitcast_fusion = f32[1024,64]{0,1:T(8,128)} fusion(bf16[64,5,768]{2,0,1:T(8,128)(2,1)S(1)} %copy.44, bf16[1024,5,768]{2,0,1:T(8,128)(2,1)} %param.9), kind=kOutput, calls=%fused_computation.11 | convolution fusion | flops 503316480 | bytes 8617984 | tf_op jit(solution)/shard_map/dot_general | solution.py:72
  124.0 5.2 %all_gather.3 = bf16[128,256]{0,1:T(8,128)(2,1)S(1)} all-gather(bf16[128,64]{0,1:T(8,128)(2,1)S(1)} %copy-done.3), channel_id=1, replica_groups=mesh['rows'=8,'modes'=4] {'modes'}, dimensions={1}, use_global_device_ids=true | all-gather | bytes 81920 | tf_op jit(solution)/shard_map/all_gather | solution.py:79
  129.3 57.7 %reduce-scatter.5.cloned.1.call-done = f32[128,64]{0,1:T(8,128)} async-done(((f32[1024,64]{0,1:T(8,128)}), f32[128,64]{0,1:T(8,128)}) %reduce-scatter.5.cloned.1.call-update) | async-done | bytes 32784 | tf_op jit(solution)/shard_map/reduce_scatter | solution.py:78
  188.9 61.3 %reduce-scatter.7.cloned.1.call-done = f32[32,64]{1,0:T(8,128)} async-done(((f32[256,64]{1,0:T(8,128)}), f32[32,64]{1,0:T(8,128)}) %reduce-scatter.7.cloned.1.call-update) | async-done | bytes 8208
  (49 shorter events, 8.3 us)
Async XLA Ops:
  7.2 179.8 %reduce-scatter.5.cloned.1.call-start = ((), (), s32[]{:S(2)}) async-start(), calls=%async_computation.2 | async-start | bytes 294912 | tf_op jit(solution)/shard_map/reduce_scatter | solution.py:78
  7.2 5.2 %collective-permute-start = (bf16[1,128,64]{1,2,0:T(8,128)(2,1)}, bf16[1,128,64]{1,2,0:T(8,128)(2,1)S(1)}, u32[]{:S(2)}, u32[]{:S(2)}) collective-permute-start(bf16[1,128,64]{1,2,0:T(8,128)(2,1)} %bitcast.73), channel_id=1, source_target_pairs={{0,4},{4,0},{8,12},{12,8},{16,20},{20,16},{24,28},{28,24},{1,5},{5... | collective-permute-start | bytes 49160 | tf_op jit(solution)/shard_map/ppermute | solution.py:18
  13.2 13.2 %collective-permute-start.1 = (bf16[2,128,64]{1,2,0:T(8,128)(2,1)S(1)}, bf16[2,128,64]{1,2,0:T(8,128)(2,1)S(1)}, u32[]{:S(2)}, u32[]{:S(2)}) collective-permute-start(bf16[2,128,64]{1,2,0:T(8,128)(2,1)S(1)} %get-tuple-element.11), channel_id=1, source_target_pairs={{0,8},{4,12},{8,0},{12,4},{16,24},{20,28},{24,16},{28,20},{1,9},{5... | collective-permute-start | bytes 98312 | tf_op jit(solution)/shard_map/ppermute | solution.py:18
  26.4 5.6 %collective-permute-start.2 = (bf16[4,128,64]{1,2,0:T(8,128)(2,1)S(1)}, bf16[4,128,64]{1,2,0:T(8,128)(2,1)S(1)}, u32[]{:S(2)}, u32[]{:S(2)}) collective-permute-start(bf16[4,128,64]{1,2,0:T(8,128)(2,1)S(1)} %bitcast.71), channel_id=1, source_target_pairs={{0,16},{4,20},{8,24},{12,28},{16,0},{20,4},{24,8},{28,12},{1,17},{... | collective-permute-start | bytes 196616 | tf_op jit(solution)/shard_map/ppermute | solution.py:18
  37.9 8.6 %copy-start.2 = (s32[6,768]{1,0:T(8,128)S(1)}, s32[6,768]{1,0:T(8,128)}, u32[]{:S(2)}) copy-start(s32[6,768]{1,0:T(8,128)} %param.14) | copy-start | bytes 55300
  39.0 14.3 %copy-start = (bf16[64,5,768]{0,1,2:T(8,128)(2,1)}, bf16[64,5,768]{0,1,2:T(8,128)(2,1)S(1)}, u32[]{:S(2)}) copy-start(bf16[64,5,768]{0,1,2:T(8,128)(2,1)S(1)} %copy.34) | copy-start | bytes 1474564
  41.4 13.8 %collective-permute-start.3 = (bf16[64,5,256]{2,0,1:T(8,128)(2,1)S(1)}, bf16[64,5,256]{2,0,1:T(8,128)(2,1)S(1)}, u32[]{:S(2)}, u32[]{:S(2)}) collective-permute-start(bf16[64,5,256]{2,0,1:T(8,128)(2,1)S(1)} %get-tuple-element.8), channel_id=1, source_target_pairs={{0,4},{4,8},{8,12},{12,16},{16,20},{20,24},{24,28},{1,5},{5,9},{9,... | collective-permute-start | bytes 491528 | tf_op jit(solution)/shard_map/ppermute | solution.py:32
  45.1 10.1 %collective-permute-start.4 = (bf16[64,5,256]{2,0,1:T(8,128)(2,1)S(1)}, bf16[64,5,256]{2,0,1:T(8,128)(2,1)}, u32[]{:S(2)}, u32[]{:S(2)}) collective-permute-start(bf16[64,5,256]{2,0,1:T(8,128)(2,1)S(1)} %get-tuple-element.9), channel_id=1, source_target_pairs={{4,0},{8,4},{12,8},{16,12},{20,16},{24,20},{28,24},{5,1},{9,5},{13... | collective-permute-start | bytes 491528 | tf_op jit(solution)/shard_map/ppermute | solution.py:32
  46.6 6.7 %copy-start.4 = (bf16[5,5,768]{2,1,0:T(8,128)(2,1)S(1)}, bf16[5,5,768]{2,1,0:T(8,128)(2,1)}, u32[]{:S(2)}) copy-start(bf16[5,5,768]{2,1,0:T(8,128)(2,1)} %param.12) | copy-start | bytes 115204
  117.3 6.6 %copy-start.1 = (bf16[64,5,768]{2,0,1:T(8,128)(2,1)}, bf16[64,5,768]{2,0,1:T(8,128)(2,1)S(1)}, u32[]{:S(2)}) copy-start(bf16[64,5,768]{2,0,1:T(8,128)(2,1)S(1)} %copy.44) | copy-start | bytes 1474564
  117.3 6.7 %copy-start.3 = (bf16[128,64]{0,1:T(8,128)(2,1)S(1)}, bf16[128,64]{0,1:T(8,128)(2,1)}, u32[]{:S(2)}) copy-start(bf16[128,64]{0,1:T(8,128)(2,1)} %param.10) | copy-start | bytes 49156
  117.4 71.4 %copy-start.5 = (f32[256]{0:T(256)S(1)}, f32[256]{0:T(256)}, u32[]{:S(2)}) copy-start(f32[256]{0:T(256)} %param.11) | copy-start | bytes 3076
  124.0 126.2 %reduce-scatter.7.cloned.1.call-start = ((), (), s32[]{:S(2)}) async-start(), calls=%async_computation.3 | async-start | bytes 147456
Sparse Core Ops, SparseCore 0:
  124.1 62.8 reduce-scatter.4
  190.3 59.8 reduce-scatter.6
